TPU v7x, 128 devices: a whole 4x4x4 slice. The times are simulated.
128 devices in a mesh: rep: 2 (over z_lo), exp: 64 (over z_hi, x, y, core).
Axes of the slice: x: 4, y: 4, z: 4 (z_hi: 2, z_lo: 2; z = z_hi * 2 + z_lo), core: 2. Of those that a mesh axis runs over, the one named last changes fastest.
Arguments:
- tokens: bfloat16 [512, 256, 1280], P(('rep', 'exp')), may hold values from -19 to 19
- slot_params: bfloat16 [1280, 64], replicated, may hold values from -1 to 1
- expert_in: bfloat16 [64, 1280, 2560], P('exp'), may hold values from -0.15625 to 0.15625
- expert_out: bfloat16 [64, 2560, 1280], P('exp'), may hold values from -0.125 to 0.125
- grad_out: bfloat16 [512, 256, 1280], P(('rep', 'exp')), may hold values from -6 to 6
Outputs:
- grad_tokens: bfloat16 [512, 256, 1280], P(('rep', 'exp'))
- grad_params: float32 [1280, 64], replicated
- grad_expert_in: bfloat16 [64, 1280, 2560], P('exp', 'rep')
- grad_expert_out: bfloat16 [64, 2560, 1280], P('exp', 'rep')
All inputs are finite; a program needn't handle non-finite values.
Results may differ from a plain program's by a relative error of at most 0.0093.
Values may be sent and summed in bfloat16 or wider, within the bound.
A program may use at most 128 MiB of HBM per device.

v0:
```python
import math

import jax
import jax.numpy as jnp
from jax import lax
from jax.experimental import pallas as pl
from jax.experimental.pallas import tpu as pltpu
from jax.sharding import PartitionSpec as P

GELU_C = math.sqrt(2.0 / math.pi)
CUBIC = 0.044715
MESH = pl.DeviceIdType.MESH

D = 1280
F = 2560
M = 256
S = 64
B = 4
R = S * B
HALF = D // 2
BF = jnp.bfloat16
F32 = jnp.float32

NT = (((1,), (1,)), ((), ()))


def dot(a, b):
    return jnp.dot(a, b, preferred_element_type=F32)


def dot_nt(a, b):
    return lax.dot_general(a, b, NT, preferred_element_type=F32)


def pack(first, second):
    width = first.shape[1]
    a = first.reshape(R // 8, 8, width)
    g = second.reshape(R // 8, 8, width)
    low = lax.broadcasted_iota(jnp.int32, a.shape, 1) < 4
    even = jnp.where(low, a, pltpu.roll(g, 4, 1))
    odd = jnp.where(low, pltpu.roll(a, 4, 1), g)
    return even, odd


def unpack(even, odd):
    low = lax.broadcasted_iota(jnp.int32, even.shape, 1) < 4
    a = jnp.where(low, even, pltpu.roll(odd, 4, 1))
    g = jnp.where(low, pltpu.roll(even, 4, 1), odd)
    return a.reshape(R, -1), g.reshape(R, -1)


def by_parity(buf):
    return buf.reshape(S // 2, 2, 16, HALF)


def store_message(msg, p, first, second):
    even, odd = pack(first, second)
    msg = by_parity(msg)
    at = pl.ds(pl.multiple_of(p * 128, 128), 128)
    for j, v in enumerate((even, odd)):
        rows = jnp.concatenate([v[:, :, :128], v[:, :, 128:]], axis=1)
        msg[:, j, :, at] = rows.astype(BF)


def load_message(rcv, p):
    rcv = by_parity(rcv)
    at = pl.ds(pl.multiple_of(p * 128, 128), 128)
    sides = []
    for j in range(2):
        rows = rcv[:, j, :, at].astype(F32)
        sides.append(jnp.concatenate([rows[:, :8], rows[:, 8:]], axis=2))
    return unpack(sides[0], sides[1])


def gelu_both(v):
    u = v * v
    t = jnp.tanh(GELU_C * (v + CUBIC * v * u))
    half = 0.5 * (1.0 + t)
    slope = half + 0.5 * v * (1.0 - t * t) * (GELU_C * (1.0 + 3.0 * CUBIC * u))
    return half * v, slope


def kernel(
    tok_hbm, sp_hbm, win_hbm, wout_hbm, gro_hbm,
    gt_hbm, gp_hbm, gi_hbm, gw_hbm,
    tok, sp, win, wout, gro, wrep, disp, comb, dmask, cmask, dlm,
    msg, rcv, msg2, rcv2, xg, act, dh, xht, actt, ys,
    gt_st, gi_st, gw_st, gp, rs, ybuf, zbuf, gbuf,
    in_sems, out_sems, ssem, rsem, ssem2, rsem2, lsems, fsem, frsem, ar_s, ar_r, sem2,
):
    r = lax.axis_index("rep")
    e = lax.axis_index("exp")
    zh = e // 32
    x = (e // 8) % 4
    y = (e // 2) % 4
    c = e % 2

    def device(zhi, zlo, xx, yy, cc):
        return (zlo, zhi * 32 + xx * 8 + yy * 2 + cc)

    def target(i, sign):
        zb = i // 32
        return device(
            (zh + zb) % 2,
            (r + zb) % 2,
            (x + sign * ((i // 8) % 4) + 4) % 4,
            (y + sign * ((i // 2) % 4) + 4) % 4,
            (c + i) % 2,
        )

    loads = [
        pltpu.make_async_copy(src, dst, in_sems.at[n])
        for n, (src, dst) in enumerate(
            ((tok_hbm, tok), (sp_hbm, sp), (gro_hbm, gro), (win_hbm, win), (wout_hbm, wout))
        )
    ]
    for copy in loads:
        copy.start()

    row_group = [ix * 8 + ic for ix in range(4) for ic in range(2) if ix + ic > 0]
    col_group = [zb * 32 + iy * 2 for zb in range(2) for iy in range(4) if zb + iy > 0]
    barrier = pltpu.get_barrier_semaphore()
    for i in row_group + col_group:
        pl.semaphore_signal(barrier, inc=1, device_id=target(i, 1), device_id_type=MESH)
    for dev in (device(zh, 1 - r, x, y, c), device(1 - zh, r, x, y, c)):
        pl.semaphore_signal(barrier, inc=1, device_id=dev, device_id_type=MESH)

    def slot_of(i):
        zb = i // 32
        return (
            ((zh + zb) % 2) * 32
            + ((x + (i // 8) % 4) % 4) * 8
            + ((y + (i // 2) % 4) % 4) * 2
            + (c + i) % 2
        )

    row_i = lax.broadcasted_iota(jnp.int32, (R, S), 0) // B
    pick = (slot_of(row_i) == lax.broadcasted_iota(jnp.int32, (R, S), 1)).astype(F32).astype(BF)
    col_i = lax.broadcasted_iota(jnp.int32, (S, R), 1) // B
    pick_t = (slot_of(col_i) == lax.broadcasted_iota(jnp.int32, (S, R), 0)).astype(F32).astype(BF)
    image = lax.broadcasted_iota(jnp.int32, (R, M), 0) % B

    loads[1].wait()
    wrep[...] = dot_nt(pick, sp[...]).astype(BF)
    loads[0].wait()
    logits = jnp.zeros((R, M), F32)
    for b in range(B):
        logits = jnp.where(image == b, dot_nt(wrep[...], tok[b]), logits)

    top = jnp.max(logits, axis=1, keepdims=True)
    p = jnp.exp(logits - top)
    dispatch = p / jnp.sum(p, axis=1, keepdims=True)
    disp[...] = dispatch
    l3 = logits.reshape(R // 8, 8, M)
    top = jnp.max(l3, axis=0)
    top = jnp.maximum(top, pltpu.roll(top, 4, 0))
    p = jnp.exp(l3 - top[None])
    total = jnp.sum(p, axis=0)
    total = total + pltpu.roll(total, 4, 0)
    combine = (p / total[None]).reshape(R, M)
    comb[...] = combine
    for b in range(B):
        dmask[:, b * M : (b + 1) * M] = jnp.where(image == b, dispatch, 0.0).astype(BF)
        cmask[:, b * M : (b + 1) * M] = jnp.where(image == b, combine, 0.0).astype(BF)
    loads[2].wait()

    def gather_step(p, carry):
        lo = pl.ds(pl.multiple_of(p * 128, 128), 128)
        hi = pl.ds(pl.multiple_of(HALF + p * 128, 128), 128)
        rhs = jnp.concatenate([tok[:, :, lo], tok[:, :, hi]], axis=2).reshape(B * M, 256)
        first = dot(dmask[...], rhs)
        rhs = jnp.concatenate([gro[:, :, lo], gro[:, :, hi]], axis=2).reshape(B * M, 256)
        second = dot(cmask[...], rhs)
        store_message(msg, p, first, second)
        return carry

    lax.fori_loop(0, 5, gather_step, 0)

    pl.semaphore_wait(barrier, 16)
    for i in row_group:
        pl.semaphore_signal(sem2, inc=1, device_id=target(i, 1), device_id_type=MESH)
    pl.semaphore_wait(sem2, 7)

    def send_all(src, dst, ssem, rsem, sign):
        def body(k, carry):
            i = (k * 29) % 64
            pltpu.make_async_remote_copy(
                src_ref=src.at[i],
                dst_ref=dst.at[i],
                send_sem=ssem,
                recv_sem=rsem,
                device_id=target(i, sign),
                device_id_type=MESH,
            ).start()
            return carry

        lax.fori_loop(1, 64, body, 0)

    def wait_63(buf, sem):
        part = buf.at[pl.ds(1, S - 1)]
        pltpu.make_async_copy(part, part, sem).wait()

    send_all(msg, rcv, ssem, rsem, 1)
    own = pltpu.make_async_copy(msg.at[0], rcv.at[0], lsems.at[0])
    own.start()
    loads[3].wait()
    loads[4].wait()
    own.wait()
    wait_63(rcv, rsem)

    def unpack_step(p, carry):
        first, second = load_message(rcv, p)
        for h in range(2):
            at = pl.ds(pl.multiple_of(h * HALF + p * 128, 128), 128)
            xg[0, 0, :, at] = first[:, h * 128 : (h + 1) * 128].astype(BF)
            xg[0, 1, :, at] = second[:, h * 128 : (h + 1) * 128].astype(BF)
        return carry

    lax.fori_loop(0, 5, unpack_step, 0)

    forward = pltpu.make_async_remote_copy(
        src_ref=xg.at[0],
        dst_ref=xg.at[1],
        send_sem=fsem,
        recv_sem=frsem,
        device_id=(1 - r, e),
        device_id_type=MESH,
    )
    forward.start()

    def hidden(side):
        def step(j, carry):
            at = pl.ds(pl.multiple_of(j * 256, 256), 256)
            pre = dot(xg[side, 0], win[:, at])
            d_act = dot_nt(xg[side, 1], wout[at, :])
            value, slope = gelu_both(pre)
            act[side, :, at] = value.astype(BF)
            dh[side, :, at] = (d_act * slope).astype(BF)
            return carry

        lax.fori_loop(0, F // 256, step, 0)

    hidden(0)

    def back_step(p, carry):
        lo = pl.ds(pl.multiple_of(p * 128, 128), 128)
        hi = pl.ds(pl.multiple_of(HALF + p * 128, 128), 128)
        first = dot(act[0], jnp.concatenate([wout[:, lo], wout[:, hi]], axis=1))
        second = dot_nt(dh[0], jnp.concatenate([win[lo, :], win[hi, :]], axis=0))
        store_message(msg2, p, first, second)
        return carry

    lax.fori_loop(0, 5, back_step, 0)
    send_all(msg2, rcv2, ssem2, rsem2, -1)
    own = pltpu.make_async_copy(msg2.at[0], rcv2.at[0], lsems.at[1])
    own.start()

    def grads(side):
        my_cols = pl.ds(pl.multiple_of(r * HALF, 128), HALF)
        my_hidden = pl.ds(pl.multiple_of(r * (F // 2), 256), F // 2)
        xht[...] = xg[side, 0, :, my_cols].T
        actt[...] = act[side, :, my_hidden].T

        def in_step(j, carry):
            at = pl.ds(pl.multiple_of(j * 256, 256), 256)
            term = dot(xht[...], dh[side, :, at])
            if side == 1:
                term = term + gi_st[:, at].astype(F32)
            gi_st[:, at] = term.astype(BF)
            return carry

        lax.fori_loop(0, F // 256, in_step, 0)

        def out_step(j, carry):
            at = pl.ds(pl.multiple_of(j * 256, 256), 256)
            term = dot(actt[...], xg[side, 1, :, at])
            if side == 1:
                term = term + gw_st[:, at].astype(F32)
            gw_st[:, at] = term.astype(BF)
            return carry

        lax.fori_loop(0, D // 256, out_step, 0)

    grads(0)
    own.wait()
    wait_63(rcv2, rsem2)

    def unpack_back(p, carry):
        first, second = load_message(rcv2, p)
        for h in range(2):
            at = pl.ds(pl.multiple_of(h * HALF + p * 128, 128), 128)
            ys[0, :, at] = first[:, h * 128 : (h + 1) * 128].astype(BF)
            ys[1, :, at] = second[:, h * 128 : (h + 1) * 128].astype(BF)
        return carry

    lax.fori_loop(0, 5, unpack_back, 0)

    d_comb = jnp.zeros((R, M), F32)
    d_disp = jnp.zeros((R, M), F32)
    for b in range(B):
        d_comb = jnp.where(image == b, dot_nt(ys[0], gro[b]), d_comb)
        d_disp = jnp.where(image == b, dot_nt(ys[1], tok[b]), d_disp)
    combine = comb[...].reshape(R // 8, 8, M)
    d_comb = d_comb.reshape(R // 8, 8, M)
    total = jnp.sum(combine * d_comb, axis=0)
    total = total + pltpu.roll(total, 4, 0)
    d_logits = (combine * (d_comb - total[None])).reshape(R, M)
    dispatch = disp[...]
    d_logits = d_logits + dispatch * (
        d_disp - jnp.sum(dispatch * d_disp, axis=1, keepdims=True)
    )
    for b in range(B):
        dlm[:, b * M : (b + 1) * M] = jnp.where(image == b, d_logits, 0.0).astype(BF)
    per_slot = dot(pick_t, dlm[...]).astype(BF)

    for j in range(D // 256):
        at = slice(j * 256, (j + 1) * 256)
        rhs = tok[:, :, at].reshape(B * M, 256)
        gp[:, :, at] = dot(per_slot, rhs).reshape(8, 8, 256)

    line = x * 2 + c
    zc = zh * 2 + r

    def line_member(d):
        return device(zh, r, (x + d // 2) % 4, y, (c + d) % 2)

    def line_index(d):
        return ((x + d // 2) % 4) * 2 + (c + d) % 2

    def remote(src, dst, phase, dev):
        return pltpu.make_async_remote_copy(
            src_ref=src,
            dst_ref=dst,
            send_sem=ar_s.at[phase],
            recv_sem=ar_r.at[phase],
            device_id=dev,
            device_id_type=MESH,
        )

    def wait_parts(buf, count, sem):
        part = buf.at[pl.ds(0, count)]
        pltpu.make_async_copy(part, part, sem).wait()

    def tokens_grad(b):
        at = slice(b * M, (b + 1) * M)
        left = jnp.concatenate([dmask[:, at], dlm[:, at]], axis=0).T
        for j in range(D // 256):
            cols = slice(j * 256, (j + 1) * 256)
            right = jnp.concatenate([ys[1, :, cols], wrep[:, cols]], axis=0)
            gt_st[b, :, cols] = dot(left, right).astype(BF)
        copy = pltpu.make_async_copy(gt_st.at[b], gt_hbm.at[b], out_sems.at[b])
        copy.start()
        return copy

    stores = []
    for d in range(1, 8):
        remote(gp.at[line_index(d)], rs.at[line], 0, line_member(d)).start()
    rs[line] = gp[line]
    stores.append(tokens_grad(0))
    stores.append(tokens_grad(1))
    wait_parts(rs, 7, ar_r.at[0])
    ybuf[y] = jnp.sum(rs[...], axis=0)
    for d in range(1, 4):
        remote(ybuf.at[y], ybuf.at[y], 1, device(zh, r, x, (y + d) % 4, c)).start()
    stores.append(tokens_grad(2))
    stores.append(tokens_grad(3))
    wait_parts(ybuf, 3, ar_r.at[1])
    zbuf[zc] = (ybuf[0] + ybuf[1]) + (ybuf[2] + ybuf[3])
    for dh_, dl_ in ((0, 1), (1, 0), (1, 1)):
        dev = device((zh + dh_) % 2, (r + dl_) % 2, x, y, c)
        remote(zbuf.at[zc], zbuf.at[zc], 2, dev).start()

    forward.wait()
    hidden(1)
    wait_parts(zbuf, 3, ar_r.at[2])
    gbuf[line] = (zbuf[0] + zbuf[1]) + (zbuf[2] + zbuf[3])
    for d in range(1, 8):
        remote(gbuf.at[line], gbuf.at[line], 3, line_member(d)).start()
    grads(1)
    for n, (src, dst) in enumerate(((gi_st, gi_hbm), (gw_st, gw_hbm))):
        copy = pltpu.make_async_copy(src, dst, out_sems.at[4 + n])
        copy.start()
        stores.append(copy)
    wait_parts(gbuf, 7, ar_r.at[3])
    copy = pltpu.make_async_copy(gbuf, gp_hbm, out_sems.at[6])
    copy.start()
    stores.append(copy)

    wait_63(msg, ssem)
    wait_63(msg2, ssem2)
    wait_parts(rs, 7, ar_s.at[0])
    wait_parts(ybuf, 3, ar_s.at[1])
    wait_parts(zbuf, 3, ar_s.at[2])
    wait_parts(gbuf, 7, ar_s.at[3])
    for copy in stores:
        copy.wait()


def body(tokens, slot_params, expert_in, expert_out, grad_out):
    vm = pltpu.VMEM
    dma = pltpu.SemaphoreType.DMA
    scratch = [
        vm((B, M, D), BF), vm((D, S), BF), vm((D, F), BF), vm((F, D), BF), vm((B, M, D), BF),
        vm((R, D), BF), vm((R, M), F32), vm((R, M), F32),
        vm((R, B * M), BF), vm((R, B * M), BF), vm((R, B * M), BF),
        vm((S, 16, HALF), BF), vm((S, 16, HALF), BF),
        vm((S, 16, HALF), BF), vm((S, 16, HALF), BF),
        vm((2, 2, R, D), BF), vm((2, R, F), BF), vm((2, R, F), BF),
        vm((HALF, R), BF), vm((F // 2, R), BF), vm((2, R, D), BF),
        vm((B, M, D), BF), vm((HALF, F), BF), vm((F // 2, D), BF),
        vm((8, 8, D), F32), vm((8, 8, D), F32), vm((4, 8, D), F32), vm((4, 8, D), F32),
        vm((8, 8, D), F32),
        dma((5,)), dma((7,)), dma, dma, dma, dma, dma((2,)), dma, dma, dma((4,)), dma((4,)),
        pltpu.SemaphoreType.REGULAR,
    ]
    anywhere = pl.BlockSpec(memory_space=pl.ANY)
    gt, gp, gi, gw = pl.pallas_call(
        kernel,
        out_shape=(
            jax.ShapeDtypeStruct((B, M, D), BF),
            jax.ShapeDtypeStruct((8, 8, D), F32),
            jax.ShapeDtypeStruct((HALF, F), BF),
            jax.ShapeDtypeStruct((F // 2, D), BF),
        ),
        in_specs=[anywhere] * 5,
        out_specs=(anywhere,) * 4,
        scratch_shapes=scratch,
        compiler_params=pltpu.CompilerParams(
            collective_id=0, has_side_effects=True, vmem_limit_bytes=60 << 20
        ),
    )(tokens, slot_params, expert_in[0], expert_out[0], grad_out)
    return gt, gp.reshape(S, D).T, gi[None], gw[None]


def solution(mesh):
    in_specs = (
        P(("rep", "exp"), None, None),
        P(),
        P("exp", None, None),
        P("exp", None, None),
        P(("rep", "exp"), None, None),
    )
    out_specs = (P(("rep", "exp"), None, None), P(), P("exp", "rep", None), P("exp", "rep", None))
    return jax.shard_map(body, mesh=mesh, in_specs=in_specs, out_specs=out_specs, check_vma=False)
```

profile of v0, /device:TPU:1, one launch (start us, length us, event | category | flops | bytes accessed | tf_op | source)
XLA Modules:
  0.0 98.4 jit_solution(15261465013494209516)
XLA Ops:
  0.6 1.8 %copy.9.sp_hbm = bf16[1280,64]{1,0:T(8,128)(2,1)} copy(bf16[1280,64]{0,1:T(8,128)(2,1)} %param.6) | data formatting | bytes 327680 | tf_op args[1]
  2.4 86.9 %shard_map.84 = (bf16[4,256,1280]{2,1,0:T(8,128)(2,1)}, f32[8,8,1280]{2,1,0:T(8,128)}, bf16[640,2560]{1,0:T(8,128)(2,1)}, bf16[1280,1280]{1,0:T(8,128)(2,1)}) custom-call(bf16[4,256,1280]{2,1,0:T(8,128)(2,1)} %tok_hbm.1, bf16[1280,64]{1,0:T(8,128)(2,1)} %copy.9.sp_hbm, bf16[1280,2560]{1,0:T(8,128)(2,1)} %bitcast.7, bf16[2560,1280]{1,0:T(8,128)(2,1)} %bitcast.8, ...), custom_call_target="tpu_custom_call" | custom-call | tf_op jit(solution)/shard_map/pallas_call | solution.py:417
  89.3 0.0 copy-start.2
  89.3 0.0 copy-start.1
  89.3 3.6 %copy.14 = bf16[4,256,1280]{2,1,0:T(8,128)(2,1)} copy(bf16[4,256,1280]{2,1,0:T(8,128)(2,1)} %get-tuple-element.16) | data formatting | bytes 5242880
  92.9 0.0 copy-done.2
  92.9 0.7 copy.15
  93.6 0.0 copy-done.1
  93.6 0.0 copy-start
  93.6 1.7 %copy.16 = bf16[1,640,2560]{2,1,0:T(8,128)(2,1)} copy(bf16[1,640,2560]{2,1,0:T(8,128)(2,1)S(1)} %bitcast.10) | data formatting | bytes 6553600
  95.3 1.4 %copy-done = bf16[1280,1280]{1,0:T(8,128)(2,1)S(1)} copy-done((bf16[1280,1280]{1,0:T(8,128)(2,1)S(1)}, bf16[1280,1280]{1,0:T(8,128)(2,1)}, u32[]{:S(2)}) %copy-start) | copy-done | bytes 3276824
  96.7 1.7 %copy.17 = bf16[1,1280,1280]{2,1,0:T(8,128)(2,1)} copy(bf16[1,1280,1280]{2,1,0:T(8,128)(2,1)S(1)} %bitcast.9) | data formatting | bytes 6553600
Async XLA Ops:
  89.3 3.6 %copy-start.2 = (f32[8,8,1280]{2,1,0:T(8,128)S(1)}, f32[8,8,1280]{2,1,0:T(8,128)}, u32[]{:S(2)}) copy-start(f32[8,8,1280]{2,1,0:T(8,128)} %get-tuple-element.9) | copy-start | bytes 983044
  89.3 4.3 %copy-start.1 = (bf16[640,2560]{1,0:T(8,128)(2,1)S(1)}, bf16[640,2560]{1,0:T(8,128)(2,1)}, u32[]{:S(2)}) copy-start(bf16[640,2560]{1,0:T(8,128)(2,1)} %get-tuple-element.10) | copy-start | bytes 9830404
  93.6 3.1 %copy-start = (bf16[1280,1280]{1,0:T(8,128)(2,1)S(1)}, bf16[1280,1280]{1,0:T(8,128)(2,1)}, u32[]{:S(2)}) copy-start(bf16[1280,1280]{1,0:T(8,128)(2,1)} %get-tuple-element.11) | copy-start | bytes 9830404
where the time goes:
time: 98.6 us; the launch traced here: 98.4 us
  Pallas kernels  86.9 us (88%)
  local copies, waits for them, and re-layouts  10.9 us (11%)
    pallas_call x1, Pallas kernels, body(): pl.pallas_call(kernel, out_shape=(jax.ShapeDtypeStruct((B, M, D), BF), ja...  86.9 us
    unnamed x11, local copies, waits for them, and re-layouts  10.9 us

commit v1 on v0

v1 whole, which is shorter than its diff:
```python
import math

import jax
import jax.numpy as jnp
from jax import lax
from jax.experimental import pallas as pl
from jax.experimental.pallas import tpu as pltpu
from jax.sharding import PartitionSpec as P

GELU_C = math.sqrt(2.0 / math.pi)
CUBIC = 0.044715
MESH = pl.DeviceIdType.MESH

D = 1280
F = 2560
M = 256
S = 64
HS = S // 2
B = 4
R = S * B
HR = R // 2
HALF = D // 2
BF = jnp.bfloat16
F32 = jnp.float32

NT = (((1,), (1,)), ((), ()))


def dot(a, b):
    return jnp.dot(a, b, preferred_element_type=F32)


def dot_nt(a, b):
    return lax.dot_general(a, b, NT, preferred_element_type=F32)


def by_parity(buf, half):
    return buf.at[pl.ds(half * HS, HS)].reshape(HS // 2, 2, 16, HALF)


def pack(first, second):
    rows, width = first.shape
    a = first.reshape(rows // 8, 8, width)
    g = second.reshape(rows // 8, 8, width)
    low = lax.broadcasted_iota(jnp.int32, a.shape, 1) < 4
    even = jnp.where(low, a, pltpu.roll(g, 4, 1))
    odd = jnp.where(low, pltpu.roll(a, 4, 1), g)
    return even, odd


def unpack(even, odd):
    rows = even.shape[0] * 8
    low = lax.broadcasted_iota(jnp.int32, even.shape, 1) < 4
    a = jnp.where(low, even, pltpu.roll(odd, 4, 1))
    g = jnp.where(low, pltpu.roll(even, 4, 1), odd)
    return a.reshape(rows, -1), g.reshape(rows, -1)


def columns(p):
    return slice(p * 128, (p + 1) * 128), slice(HALF + p * 128, HALF + (p + 1) * 128)


def store_message(msg, half, p, first, second):
    even, odd = pack(first, second)
    msg = by_parity(msg, half)
    for j, v in enumerate((even, odd)):
        rows = jnp.concatenate([v[:, :, :128], v[:, :, 128:]], axis=1)
        msg[:, j, :, columns(p)[0]] = rows.astype(BF)


def load_message(rcv, half, p):
    rcv = by_parity(rcv, half)
    sides = []
    for j in range(2):
        rows = rcv[:, j, :, columns(p)[0]].astype(F32)
        sides.append(jnp.concatenate([rows[:, :8], rows[:, 8:]], axis=2))
    return unpack(sides[0], sides[1])


def gelu_both(v):
    u = v * v
    t = jnp.tanh(GELU_C * (v + CUBIC * v * u))
    half = 0.5 * (1.0 + t)
    slope = half + 0.5 * v * (1.0 - t * t) * (GELU_C * (1.0 + 3.0 * CUBIC * u))
    return half * v, slope


def kernel(
    tok_hbm, sp_hbm, win_hbm, wout_hbm, gro_hbm,
    gt_out, gp_out, gi_out, gw_out,
    tok, sp, win, wout, gro, wrep, disp, comb, dmask, cmask, dlm,
    msg, rcv, msg2, rcv2, xg, act, dh, xht, actt, ys, gp, rs, ybuf, zbuf,
    in_sems, ssem, rsem, ssem2, rsem2, lsems, fsem, frsem, ar_s, ar_r, sem2,
):
    r = lax.axis_index("rep")
    e = lax.axis_index("exp")
    zh = e // 32
    x = (e // 8) % 4
    y = (e // 2) % 4
    c = e % 2

    def device(zhi, zlo, xx, yy, cc):
        return (zlo, zhi * 32 + xx * 8 + yy * 2 + cc)

    def target(i, sign):
        zb = (i // 16) % 2
        return device(
            (zh + zb) % 2,
            (r + zb) % 2,
            (x + sign * ((i // 4) % 4) + 4) % 4,
            (y + sign * (i % 4) + 4) % 4,
            (c + i // 32) % 2,
        )

    loads = [
        pltpu.make_async_copy(src, dst, in_sems.at[n])
        for n, (src, dst) in enumerate(
            ((tok_hbm, tok), (sp_hbm, sp), (gro_hbm, gro), (win_hbm, win), (wout_hbm, wout))
        )
    ]
    for copy in loads:
        copy.start()

    row_group = [ic * 32 + ix * 4 for ic in range(2) for ix in range(4) if ic + ix > 0]
    col_group = [zb * 16 + iy for zb in range(2) for iy in range(4) if zb + iy > 0]
    barrier = pltpu.get_barrier_semaphore()
    for i in row_group + col_group:
        pl.semaphore_signal(barrier, inc=1, device_id=target(i, 1), device_id_type=MESH)
    for dev in (device(zh, 1 - r, x, y, c), device(1 - zh, r, x, y, c)):
        pl.semaphore_signal(barrier, inc=1, device_id=dev, device_id_type=MESH)

    def slot_of(i):
        zb = (i // 16) % 2
        return (
            ((zh + zb) % 2) * 32
            + ((x + (i // 4) % 4) % 4) * 8
            + ((y + i % 4) % 4) * 2
            + (c + i // 32) % 2
        )

    row_i = lax.broadcasted_iota(jnp.int32, (R, S), 0) // B
    pick = (slot_of(row_i) == lax.broadcasted_iota(jnp.int32, (R, S), 1)).astype(F32).astype(BF)
    col_i = lax.broadcasted_iota(jnp.int32, (S, R), 1) // B
    pick_t = (slot_of(col_i) == lax.broadcasted_iota(jnp.int32, (S, R), 0)).astype(F32).astype(BF)
    image = lax.broadcasted_iota(jnp.int32, (R, M), 0) % B

    loads[1].wait()
    wrep[...] = dot(pick, sp[...]).astype(BF)
    loads[0].wait()
    logits = jnp.zeros((R, M), F32)
    for b in range(B):
        logits = jnp.where(image == b, dot_nt(wrep[...], tok[b]), logits)

    top = jnp.max(logits, axis=1, keepdims=True)
    p = jnp.exp(logits - top)
    dispatch = p / jnp.sum(p, axis=1, keepdims=True)
    disp[...] = dispatch
    l3 = logits.reshape(R // 8, 8, M)
    top = jnp.max(l3, axis=0)
    top = jnp.maximum(top, pltpu.roll(top, 4, 0))
    p = jnp.exp(l3 - top[None])
    total = jnp.sum(p, axis=0)
    total = total + pltpu.roll(total, 4, 0)
    combine = (p / total[None]).reshape(R, M)
    comb[...] = combine
    for b in range(B):
        dmask[:, b * M : (b + 1) * M] = jnp.where(image == b, dispatch, 0.0).astype(BF)
        cmask[:, b * M : (b + 1) * M] = jnp.where(image == b, combine, 0.0).astype(BF)
    loads[2].wait()

    pl.semaphore_wait(barrier, 16)
    for i in row_group:
        pl.semaphore_signal(sem2, inc=1, device_id=target(i, 1), device_id_type=MESH)

    def gather(half):
        rows = slice(half * HR, (half + 1) * HR)
        for p in range(5):
            lo, hi = columns(p)
            rhs = jnp.concatenate([tok[:, :, lo], tok[:, :, hi]], axis=2).reshape(B * M, 256)
            first = dot(dmask[rows, :], rhs)
            rhs = jnp.concatenate([gro[:, :, lo], gro[:, :, hi]], axis=2).reshape(B * M, 256)
            second = dot(cmask[rows, :], rhs)
            store_message(msg, half, p, first, second)

    def send_half(half, src, dst, ssem, rsem, sign):
        def body(k, carry):
            i = half * HS + (k * 13) % HS
            pltpu.make_async_remote_copy(
                src_ref=src.at[i],
                dst_ref=dst.at[i],
                send_sem=ssem.at[half],
                recv_sem=rsem.at[half],
                device_id=target(i, sign),
                device_id_type=MESH,
            ).start()
            return carry

        lax.fori_loop(1 - half, HS, body, 0)

    def wait_half(half, buf, sem):
        part = buf.at[pl.ds(half * HS + 1 - half, HS - 1 + half)]
        pltpu.make_async_copy(part, part, sem.at[half]).wait()

    gather(0)
    pl.semaphore_wait(sem2, 7)
    send_half(0, msg, rcv, ssem, rsem, 1)
    own = pltpu.make_async_copy(msg.at[0], rcv.at[0], lsems.at[0])
    own.start()
    gather(1)
    send_half(1, msg, rcv, ssem, rsem, 1)
    loads[3].wait()
    loads[4].wait()
    own.wait()

    def hidden(side, halves):
        rows = slice(halves[0] * HR, (halves[-1] + 1) * HR)
        count = len(halves) * HR
        at_h = slice(halves[0], halves[-1] + 1)
        previous = None
        for j in range(F // 256 + 1):
            current = None
            if j < F // 256:
                at = slice(j * 256, (j + 1) * 256)
                pre = dot(xg[side, at_h, 0].reshape(count, D), win[:, at])
                d_act = dot_nt(xg[side, at_h, 1].reshape(count, D), wout[at, :])
                current = (pre, d_act, at)
            if previous is not None:
                pre, d_act, at = previous
                value, slope = gelu_both(pre)
                act[side, rows, at] = value.astype(BF)
                dh[side, rows, at] = (d_act * slope).astype(BF)
            previous = current

    forwards = []

    def expert(half):
        wait_half(half, rcv, rsem)
        for p in range(5):
            first, second = load_message(rcv, half, p)
            for h, at in enumerate(columns(p)):
                xg[0, half, 0, :, at] = first[:, h * 128 : (h + 1) * 128].astype(BF)
                xg[0, half, 1, :, at] = second[:, h * 128 : (h + 1) * 128].astype(BF)
        forward = pltpu.make_async_remote_copy(
            src_ref=xg.at[0, half],
            dst_ref=xg.at[1, half],
            send_sem=fsem.at[half],
            recv_sem=frsem.at[half],
            device_id=(1 - r, e),
            device_id_type=MESH,
        )
        forward.start()
        forwards.append(forward)
        hidden(0, (half,))
        rows = slice(half * HR, (half + 1) * HR)
        for p in range(5):
            lo, hi = columns(p)
            first = dot(act[0, rows, :], jnp.concatenate([wout[:, lo], wout[:, hi]], axis=1))
            second = dot_nt(dh[0, rows, :], jnp.concatenate([win[lo, :], win[hi, :]], axis=0))
            store_message(msg2, half, p, first, second)
        send_half(half, msg2, rcv2, ssem2, rsem2, -1)

    expert(0)
    own = pltpu.make_async_copy(msg2.at[0], rcv2.at[0], lsems.at[1])
    own.start()
    expert(1)

    my_cols = pl.ds(pl.multiple_of(r * HALF, 128), HALF)
    my_hidden = pl.ds(pl.multiple_of(r * (F // 2), 256), F // 2)

    def grad_in(side):
        xht[...] = xg[side, :, 0, :, my_cols].reshape(R, HALF).T
        for j in range(F // 256):
            at = slice(j * 256, (j + 1) * 256)
            term = dot(xht[...], dh[side, :, at])
            if side == 1:
                term = term + gi_out[:, at].astype(F32)
            gi_out[:, at] = term.astype(BF)

    def grad_out(side):
        actt[...] = act[side, :, my_hidden].T
        for j in range(D // 256):
            at = slice(j * 256, (j + 1) * 256)
            term = dot(actt[...], xg[side, :, 1, :, at].reshape(R, 256))
            if side == 1:
                term = term + gw_out[:, at].astype(F32)
            gw_out[:, at] = term.astype(BF)

    grad_in(0)
    grad_out(0)
    own.wait()
    for half in range(2):
        wait_half(half, rcv2, rsem2)
        rows = slice(half * HR, (half + 1) * HR)
        for p in range(5):
            first, second = load_message(rcv2, half, p)
            for h, at in enumerate(columns(p)):
                ys[0, rows, at] = first[:, h * 128 : (h + 1) * 128].astype(BF)
                ys[1, rows, at] = second[:, h * 128 : (h + 1) * 128].astype(BF)

    d_comb = jnp.zeros((R, M), F32)
    d_disp = jnp.zeros((R, M), F32)
    for b in range(B):
        d_comb = jnp.where(image == b, dot_nt(ys[0], gro[b]), d_comb)
        d_disp = jnp.where(image == b, dot_nt(ys[1], tok[b]), d_disp)
    combine = comb[...].reshape(R // 8, 8, M)
    d_comb = d_comb.reshape(R // 8, 8, M)
    total = jnp.sum(combine * d_comb, axis=0)
    total = total + pltpu.roll(total, 4, 0)
    d_logits = (combine * (d_comb - total[None])).reshape(R, M)
    dispatch = disp[...]
    d_logits = d_logits + dispatch * (
        d_disp - jnp.sum(dispatch * d_disp, axis=1, keepdims=True)
    )
    for b in range(B):
        dlm[:, b * M : (b + 1) * M] = jnp.where(image == b, d_logits, 0.0).astype(BF)
    per_slot = dot(pick_t, dlm[...]).astype(BF)

    for j in range(D // 256):
        at = slice(j * 256, (j + 1) * 256)
        rhs = tok[:, :, at].reshape(B * M, 256)
        gp[:, :, at] = dot(per_slot, rhs).reshape(8, 8, 256)

    line = x * 2 + c
    zc = zh * 2 + r

    def line_member(d):
        return device(zh, r, (x + d // 2) % 4, y, (c + d) % 2)

    def line_index(d):
        return ((x + d // 2) % 4) * 2 + (c + d) % 2

    def remote(src, dst, phase, dev):
        return pltpu.make_async_remote_copy(
            src_ref=src,
            dst_ref=dst,
            send_sem=ar_s.at[phase],
            recv_sem=ar_r.at[phase],
            device_id=dev,
            device_id_type=MESH,
        )

    def wait_parts(buf, count, sem):
        part = buf.at[pl.ds(0, count)]
        pltpu.make_async_copy(part, part, sem).wait()

    def tokens_grad(b):
        at = slice(b * M, (b + 1) * M)
        left = jnp.concatenate([dmask[:, at], dlm[:, at]], axis=0).T
        for j in range(D // 256):
            cols = slice(j * 256, (j + 1) * 256)
            right = jnp.concatenate([ys[1, :, cols], wrep[:, cols]], axis=0)
            gt_out[b, :, cols] = dot(left, right).astype(BF)

    for d in range(1, 8):
        remote(gp.at[line_index(d)], rs.at[line], 0, line_member(d)).start()
    rs[line] = gp[line]
    for forward in forwards:
        forward.wait()
    hidden(1, (0, 1))

    wait_parts(rs, 7, ar_r.at[0])
    ybuf[y] = jnp.sum(rs[...], axis=0)
    for d in range(1, 4):
        remote(ybuf.at[y], ybuf.at[y], 1, device(zh, r, x, (y + d) % 4, c)).start()
    grad_in(1)

    wait_parts(ybuf, 3, ar_r.at[1])
    zbuf[zc] = (ybuf[0] + ybuf[1]) + (ybuf[2] + ybuf[3])
    for dh_, dl_ in ((0, 1), (1, 0), (1, 1)):
        dev = device((zh + dh_) % 2, (r + dl_) % 2, x, y, c)
        remote(zbuf.at[zc], zbuf.at[zc], 2, dev).start()
    grad_out(1)

    wait_parts(zbuf, 3, ar_r.at[2])
    gp_out[line] = (zbuf[0] + zbuf[1]) + (zbuf[2] + zbuf[3])
    for d in range(1, 8):
        remote(gp_out.at[line], gp_out.at[line], 3, line_member(d)).start()
    for b in range(B):
        tokens_grad(b)
    wait_parts(gp_out, 7, ar_r.at[3])

    for half in range(2):
        wait_half(half, msg, ssem)
        wait_half(half, msg2, ssem2)
    wait_parts(rs, 7, ar_s.at[0])
    wait_parts(ybuf, 3, ar_s.at[1])
    wait_parts(zbuf, 3, ar_s.at[2])
    wait_parts(gp_out, 7, ar_s.at[3])


def store_kernel(*refs):
    sources, targets, sems = refs[:4], refs[4:8], refs[8]
    copies = [
        pltpu.make_async_copy(src, dst, sems.at[n])
        for n, (src, dst) in enumerate(zip(sources, targets))
    ]
    for copy in copies:
        copy.start()
    for copy in copies:
        copy.wait()


def body(tokens, slot_params, expert_in, expert_out, grad_out):
    vm = pltpu.VMEM
    dma = pltpu.SemaphoreType.DMA
    scratch = [
        vm((B, M, D), BF), vm((S, D), BF), vm((D, F), BF), vm((F, D), BF), vm((B, M, D), BF),
        vm((R, D), BF), vm((R, M), F32), vm((R, M), F32),
        vm((R, B * M), BF), vm((R, B * M), BF), vm((R, B * M), BF),
        vm((S, 16, HALF), BF), vm((S, 16, HALF), BF),
        vm((S, 16, HALF), BF), vm((S, 16, HALF), BF),
        vm((2, 2, 2, HR, D), BF), vm((2, R, F), BF), vm((2, R, F), BF),
        vm((HALF, R), BF), vm((F // 2, R), BF), vm((2, R, D), BF),
        vm((8, 8, D), F32), vm((8, 8, D), F32), vm((4, 8, D), F32), vm((4, 8, D), F32),
        dma((5,)), dma((2,)), dma((2,)), dma((2,)), dma((2,)), dma((2,)), dma((2,)), dma((2,)),
        dma((4,)), dma((4,)), pltpu.SemaphoreType.REGULAR,
    ]
    anywhere = pl.BlockSpec(memory_space=pl.ANY)
    in_vmem = pl.BlockSpec(memory_space=vm)
    shapes = (((B, M, D), BF), ((8, 8, D), F32), ((HALF, F), BF), ((F // 2, D), BF))
    results = pl.pallas_call(
        kernel,
        out_shape=tuple(vm(*shape) for shape in shapes),
        in_specs=[anywhere] * 5,
        out_specs=(in_vmem,) * 4,
        scratch_shapes=scratch,
        compiler_params=pltpu.CompilerParams(
            collective_id=0, has_side_effects=True, vmem_limit_bytes=48 << 20
        ),
    )(tokens, slot_params.T, expert_in[0], expert_out[0], grad_out)
    gt, gp, gi, gw = pl.pallas_call(
        store_kernel,
        out_shape=tuple(jax.ShapeDtypeStruct(*shape) for shape in shapes),
        in_specs=[in_vmem] * 4,
        out_specs=(anywhere,) * 4,
        scratch_shapes=[dma((4,))],
        compiler_params=pltpu.CompilerParams(vmem_limit_bytes=1 << 20),
    )(*(pltpu.with_memory_space_constraint(v, vm) for v in results))
    return gt, gp.reshape(S, D).T, gi[None], gw[None]


def solution(mesh):
    in_specs = (
        P(("rep", "exp"), None, None),
        P(),
        P("exp", None, None),
        P("exp", None, None),
        P(("rep", "exp"), None, None),
    )
    out_specs = (P(("rep", "exp"), None, None), P(), P("exp", "rep", None), P("exp", "rep", None))
    return jax.shard_map(body, mesh=mesh, in_specs=in_specs, out_specs=out_specs, check_vma=False)
```

time: 98.6 us -> 74.1 us (0.75)
  Pallas kernels: 86.9 us -> 73.2 us
  local copies, waits for them, and re-layouts: 10.9 us -> 0 us
    pallas_call x1 -> x2, Pallas kernels: 86.9 us -> 73.2 us  [the longest x1 69.4 us: body(): pl.pallas_call(kernel, out_shape=tuple((vm(*shape) for shape in shapes)),...]
    unnamed x11 -> x0, local copies, waits for them, and re-layouts: 10.9 us -> none
where the time goes in v1:
time: 74.1 us; the launch traced here: 74 us
  Pallas kernels  73.2 us (99%)
  between operations  0.82 us (1%)
    pallas_call x1, Pallas kernels, body(): pl.pallas_call(kernel, out_shape=tuple((vm(*shape) for shape in shapes)),...  69.4 us
    pallas_call x1, Pallas kernels, body(): pl.pallas_call(store_kernel, out_shape=tuple((jax.ShapeDtypeStruct(*shape...  3.79 us

profile of v1, /device:TPU:1, one launch (start us, length us, event | category | flops | bytes accessed | tf_op | source)
XLA Modules:
  0.0 74.0 jit_solution(10939821872047558409)
XLA Ops:
  0.6 69.4 %shard_map.84 = (bf16[4,256,1280]{2,1,0:T(8,128)(2,1)S(1)}, f32[8,8,1280]{2,1,0:T(8,128)S(1)}, bf16[640,2560]{1,0:T(8,128)(2,1)S(1)}, bf16[1280,1280]{1,0:T(8,128)(2,1)S(1)}) custom-call(bf16[4,256,1280]{2,1,0:T(8,128)(2,1)} %tok_hbm.1, bf16[64,1280]{1,0:T(8,128)(2,1)} %bitcast.10, bf16[1280,2560]{1,0:T(8,128)(2,1)} %bitcast.8, bf16[2560,1280]{1,0:T(8,128)(2,1)} %bitcast.9, ...), custom_call_target="tpu_custom_call" | custom-call | tf_op jit(solution)/shard_map/pallas_call | solution.py:421
  70.0 3.8 %shard_map.85 = (bf16[4,256,1280]{2,1,0:T(8,128)(2,1)}, f32[8,8,1280]{2,1,0:T(8,128)}, bf16[640,2560]{1,0:T(8,128)(2,1)}, bf16[1280,1280]{1,0:T(8,128)(2,1)}) custom-call(bf16[4,256,1280]{2,1,0:T(8,128)(2,1)S(1)} %get-tuple-element.12.refs_0_, f32[8,8,1280]{2,1,0:T(8,128)S(1)} %get-tuple-element.13.refs_1_, bf16[640,2560]{1,0:T(8,128)(2,1)S(1)} %get-tuple-element.14.refs_2_, ...), custom_call_target="tpu_custom_call" | custom-call | tf_op jit(solution)/shard_map/pallas_call | solution.py:431

commit v2 on v1

--- a/solution.py
+++ b/solution.py
@@ -23,6 +23,13 @@
 BF = jnp.bfloat16
 F32 = jnp.float32
 
+def hops(i):
+    return (i // 16) % 2 + (0, 1, 2, 1)[(i // 4) % 4] + (0, 1, 2, 1)[i % 4]
+
+
+FAR_FIRST = sorted(range(HS), key=lambda i: -hops(i))
+PIECE = 384
+
 NT = (((1,), (1,)), ((), ()))
 
 
@@ -89,7 +96,7 @@
     tok_hbm, sp_hbm, win_hbm, wout_hbm, gro_hbm,
     gt_out, gp_out, gi_out, gw_out,
     tok, sp, win, wout, gro, wrep, disp, comb, dmask, cmask, dlm,
-    msg, rcv, msg2, rcv2, xg, act, dh, xht, actt, ys, gp, rs, ybuf, zbuf,
+    msg, rcv, msg2, rcv2, xg, act, dh, xht, actt, ys, gp, cbuf, mine, rs, zbuf, whole,
     in_sems, ssem, rsem, ssem2, rsem2, lsems, fsem, frsem, ar_s, ar_r, sem2,
 ):
     r = lax.axis_index("rep")
@@ -183,19 +190,17 @@
             store_message(msg, half, p, first, second)
 
     def send_half(half, src, dst, ssem, rsem, sign):
-        def body(k, carry):
-            i = half * HS + (k * 13) % HS
-            pltpu.make_async_remote_copy(
-                src_ref=src.at[i],
-                dst_ref=dst.at[i],
-                send_sem=ssem.at[half],
-                recv_sem=rsem.at[half],
-                device_id=target(i, sign),
-                device_id_type=MESH,
-            ).start()
-            return carry
-
-        lax.fori_loop(1 - half, HS, body, 0)
+        for k in FAR_FIRST:
+            i = half * HS + k
+            if i > 0:
+                pltpu.make_async_remote_copy(
+                    src_ref=src.at[i],
+                    dst_ref=dst.at[i],
+                    send_sem=ssem.at[half],
+                    recv_sem=rsem.at[half],
+                    device_id=target(i, sign),
+                    device_id_type=MESH,
+                ).start()
 
     def wait_half(half, buf, sem):
         part = buf.at[pl.ds(half * HS + 1 - half, HS - 1 + half)]
@@ -288,6 +293,7 @@
     grad_in(0)
     grad_out(0)
     own.wait()
+    d_comb, d_disp = [], []
     for half in range(2):
         wait_half(half, rcv2, rsem2)
         rows = slice(half * HR, (half + 1) * HR)
@@ -296,12 +302,15 @@
             for h, at in enumerate(columns(p)):
                 ys[0, rows, at] = first[:, h * 128 : (h + 1) * 128].astype(BF)
                 ys[1, rows, at] = second[:, h * 128 : (h + 1) * 128].astype(BF)
-
-    d_comb = jnp.zeros((R, M), F32)
-    d_disp = jnp.zeros((R, M), F32)
-    for b in range(B):
-        d_comb = jnp.where(image == b, dot_nt(ys[0], gro[b]), d_comb)
-        d_disp = jnp.where(image == b, dot_nt(ys[1], tok[b]), d_disp)
+        of_comb = jnp.zeros((HR, M), F32)
+        of_disp = jnp.zeros((HR, M), F32)
+        for b in range(B):
+            of_comb = jnp.where(image[:HR] == b, dot_nt(ys[0, rows, :], gro[b]), of_comb)
+            of_disp = jnp.where(image[:HR] == b, dot_nt(ys[1, rows, :], tok[b]), of_disp)
+        d_comb.append(of_comb)
+        d_disp.append(of_disp)
+    d_comb = jnp.concatenate(d_comb, axis=0)
+    d_disp = jnp.concatenate(d_disp, axis=0)
     combine = comb[...].reshape(R // 8, 8, M)
     d_comb = d_comb.reshape(R // 8, 8, M)
     total = jnp.sum(combine * d_comb, axis=0)
@@ -315,19 +324,20 @@
         dlm[:, b * M : (b + 1) * M] = jnp.where(image == b, d_logits, 0.0).astype(BF)
     per_slot = dot(pick_t, dlm[...]).astype(BF)
 
-    for j in range(D // 256):
-        at = slice(j * 256, (j + 1) * 256)
-        rhs = tok[:, :, at].reshape(B * M, 256)
-        gp[:, :, at] = dot(per_slot, rhs).reshape(8, 8, 256)
-
-    line = x * 2 + c
+    for q in range(4):
+        width = min(PIECE, D - q * PIECE)
+        rhs = tok[:, :, q * PIECE : q * PIECE + width].reshape(B * M, width)
+        gp[:, :, q, :, :width] = dot(per_slot, rhs).reshape(2, 4, 8, width)
+    gp[:, :, 3, :, width:] = jnp.zeros((2, 4, 8, PIECE - width), F32)
+
     zc = zh * 2 + r
-
-    def line_member(d):
-        return device(zh, r, (x + d // 2) % 4, y, (c + d) % 2)
-
-    def line_index(d):
-        return ((x + d // 2) % 4) * 2 + (c + d) % 2
+    sibling = device(zh, r, x, y, 1 - c)
+
+    def plane(d):
+        xx, yy = (x + d // 4) % 4, (y + d % 4) % 4
+        return xx, yy, device(zh, r, xx, yy, c)
+
+    plane_far = sorted(range(1, 16), key=lambda d: -hops(d))
 
     def remote(src, dst, phase, dev):
         return pltpu.make_async_remote_copy(
@@ -351,49 +361,65 @@
             right = jnp.concatenate([ys[1, :, cols], wrep[:, cols]], axis=0)
             gt_out[b, :, cols] = dot(left, right).astype(BF)
 
-    for d in range(1, 8):
-        remote(gp.at[line_index(d)], rs.at[line], 0, line_member(d)).start()
-    rs[line] = gp[line]
+    to_core = remote(gp.at[1 - c], cbuf, 0, sibling)
+    to_core.start()
+    to_core.wait_recv()
+    mine[...] = gp[c] + cbuf[...]
+    for d in plane_far:
+        xx, yy, dev = plane(d)
+        remote(mine.at[xx, yy], rs.at[x * 4 + y], 1, dev).start()
+    rs[x * 4 + y] = mine[x, y]
     for forward in forwards:
         forward.wait()
     hidden(1, (0, 1))
 
-    wait_parts(rs, 7, ar_r.at[0])
-    ybuf[y] = jnp.sum(rs[...], axis=0)
-    for d in range(1, 4):
-        remote(ybuf.at[y], ybuf.at[y], 1, device(zh, r, x, (y + d) % 4, c)).start()
-    grad_in(1)
-
-    wait_parts(ybuf, 3, ar_r.at[1])
-    zbuf[zc] = (ybuf[0] + ybuf[1]) + (ybuf[2] + ybuf[3])
+    wait_parts(rs, 15, ar_r.at[1])
+    zbuf[zc] = jnp.sum(rs[...], axis=0)
     for dh_, dl_ in ((0, 1), (1, 0), (1, 1)):
         dev = device((zh + dh_) % 2, (r + dl_) % 2, x, y, c)
         remote(zbuf.at[zc], zbuf.at[zc], 2, dev).start()
+    grad_in(1)
     grad_out(1)
 
     wait_parts(zbuf, 3, ar_r.at[2])
-    gp_out[line] = (zbuf[0] + zbuf[1]) + (zbuf[2] + zbuf[3])
-    for d in range(1, 8):
-        remote(gp_out.at[line], gp_out.at[line], 3, line_member(d)).start()
+    total = (zbuf[0] + zbuf[1]) + (zbuf[2] + zbuf[3])
+    tall = [total[:, t * 128 : (t + 1) * 128] for t in range(3)] + [jnp.zeros((8, 128), F32)]
+    me = c * 16 + x * 4 + y
+    whole[me] = jnp.concatenate(tall, axis=0).astype(BF)
+    for d in sorted(range(1, 32), key=lambda d: -hops(d % 16)):
+        xx, yy, cc = (x + (d // 4) % 4) % 4, (y + d % 4) % 4, (c + d // 16) % 2
+        remote(whole.at[me], whole.at[me], 3, device(zh, r, xx, yy, cc)).start()
     for b in range(B):
         tokens_grad(b)
-    wait_parts(gp_out, 7, ar_r.at[3])
+    wait_parts(whole, 31, ar_r.at[3])
+    for ch in range(2):
+        for xy in range(16):
+            piece = whole[ch * 16 + xy].astype(F32)
+            for t in range(3):
+                lane = (xy % 4) * PIECE + t * 128
+                if lane < D:
+                    gp_out[ch * 4 + xy // 4, :, lane : lane + 128] = piece[t * 8 : t * 8 + 8]
 
     for half in range(2):
         wait_half(half, msg, ssem)
         wait_half(half, msg2, ssem2)
-    wait_parts(rs, 7, ar_s.at[0])
-    wait_parts(ybuf, 3, ar_s.at[1])
+    to_core.wait_send()
+    wait_parts(rs, 15, ar_s.at[1])
     wait_parts(zbuf, 3, ar_s.at[2])
-    wait_parts(gp_out, 7, ar_s.at[3])
+    wait_parts(whole, 31, ar_s.at[3])
 
 
 def store_kernel(*refs):
     sources, targets, sems = refs[:4], refs[4:8], refs[8]
-    copies = [
-        pltpu.make_async_copy(src, dst, sems.at[n])
-        for n, (src, dst) in enumerate(zip(sources, targets))
-    ]
+    copies = []
+    for src, dst in zip(sources, targets):
+        if len(src.shape) == 3:
+            step = 1 if src.shape[0] == B else src.shape[0]
+            parts = [pl.ds(n, step) for n in range(0, src.shape[0], step)]
+        else:
+            parts = [pl.ds(n, 160) for n in range(0, src.shape[0], 160)]
+        for part in parts:
+            copies.append(pltpu.make_async_copy(src.at[part], dst.at[part], sems.at[len(copies)]))
     for copy in copies:
         copy.start()
     for copy in copies:
@@ -411,7 +437,8 @@
         vm((S, 16, HALF), BF), vm((S, 16, HALF), BF),
         vm((2, 2, 2, HR, D), BF), vm((2, R, F), BF), vm((2, R, F), BF),
         vm((HALF, R), BF), vm((F // 2, R), BF), vm((2, R, D), BF),
-        vm((8, 8, D), F32), vm((8, 8, D), F32), vm((4, 8, D), F32), vm((4, 8, D), F32),
+        vm((2, 4, 4, 8, PIECE), F32), vm((4, 4, 8, PIECE), F32), vm((4, 4, 8, PIECE), F32),
+        vm((16, 8, PIECE), F32), vm((4, 8, PIECE), F32), vm((32, 32, 128), BF),
         dma((5,)), dma((2,)), dma((2,)), dma((2,)), dma((2,)), dma((2,)), dma((2,)), dma((2,)),
         dma((4,)), dma((4,)), pltpu.SemaphoreType.REGULAR,
     ]
@@ -433,7 +460,7 @@
         out_shape=tuple(jax.ShapeDtypeStruct(*shape) for shape in shapes),
         in_specs=[in_vmem] * 4,
         out_specs=(anywhere,) * 4,
-        scratch_shapes=[dma((4,))],
+        scratch_shapes=[dma((17,))],
         compiler_params=pltpu.CompilerParams(vmem_limit_bytes=1 << 20),
     )(*(pltpu.with_memory_space_constraint(v, vm) for v in results))
     return gt, gp.reshape(S, D).T, gi[None], gw[None]

time: 74.1 us -> 68.9 us (0.930)
  Pallas kernels: 73.2 us -> 68 us
    pallas_call x1, Pallas kernels: 69.4 us -> 64.2 us  [body(): pl.pallas_call(kernel, out_shape=tuple((vm(*shape) for shape in shapes)),...]
where the time goes in v2:
time: 68.9 us; the launch traced here: 68.8 us
  Pallas kernels  68 us (99%)
  between operations  0.82 us (1%)
    pallas_call x1, Pallas kernels, body(): pl.pallas_call(kernel, out_shape=tuple((vm(*shape) for shape in shapes)),...  64.2 us
    pallas_call x1, Pallas kernels, body(): pl.pallas_call(store_kernel, out_shape=tuple((jax.ShapeDtypeStruct(*shape...  3.77 us

profile of v2, /device:TPU:1, one launch (start us, length us, event | category | flops | bytes accessed | tf_op | source)
XLA Modules:
  0.0 68.8 jit_solution(16497441090718851297)
XLA Ops:
  0.6 64.2 %shard_map.84 = (bf16[4,256,1280]{2,1,0:T(8,128)(2,1)S(1)}, f32[8,8,1280]{2,1,0:T(8,128)S(1)}, bf16[640,2560]{1,0:T(8,128)(2,1)S(1)}, bf16[1280,1280]{1,0:T(8,128)(2,1)S(1)}) custom-call(bf16[4,256,1280]{2,1,0:T(8,128)(2,1)} %tok_hbm.1, bf16[64,1280]{1,0:T(8,128)(2,1)} %bitcast.10, bf16[1280,2560]{1,0:T(8,128)(2,1)} %bitcast.8, bf16[2560,1280]{1,0:T(8,128)(2,1)} %bitcast.9, ...), custom_call_target="tpu_custom_call" | custom-call | tf_op jit(solution)/shard_map/pallas_call | solution.py:448
  64.9 3.8 %shard_map.85 = (bf16[4,256,1280]{2,1,0:T(8,128)(2,1)}, f32[8,8,1280]{2,1,0:T(8,128)}, bf16[640,2560]{1,0:T(8,128)(2,1)}, bf16[1280,1280]{1,0:T(8,128)(2,1)}) custom-call(bf16[4,256,1280]{2,1,0:T(8,128)(2,1)S(1)} %get-tuple-element.12.refs_0_, f32[8,8,1280]{2,1,0:T(8,128)S(1)} %get-tuple-element.13.refs_1_, bf16[640,2560]{1,0:T(8,128)(2,1)S(1)} %get-tuple-element.14.refs_2_, ...), custom_call_target="tpu_custom_call" | custom-call | tf_op jit(solution)/shard_map/pallas_call | solution.py:458

commit v3 on v2

--- a/solution.py
+++ b/solution.py
@@ -125,7 +125,7 @@
             ((tok_hbm, tok), (sp_hbm, sp), (gro_hbm, gro), (win_hbm, win), (wout_hbm, wout))
         )
     ]
-    for copy in loads:
+    for copy in loads[:3]:
         copy.start()
 
     row_group = [ic * 32 + ix * 4 for ic in range(2) for ix in range(4) if ic + ix > 0]
@@ -174,6 +174,8 @@
         dmask[:, b * M : (b + 1) * M] = jnp.where(image == b, dispatch, 0.0).astype(BF)
         cmask[:, b * M : (b + 1) * M] = jnp.where(image == b, combine, 0.0).astype(BF)
     loads[2].wait()
+    for copy in loads[3:]:
+        copy.start()
 
     pl.semaphore_wait(barrier, 16)
     for i in row_group:

time: 68.9 us -> 68.9 us (level)
  no operation moved by 1% of the time
where the time goes in v3:
time: 68.9 us; the launch traced here: 68.8 us
  Pallas kernels  68 us (99%)
  between operations  0.82 us (1%)
    pallas_call x1, Pallas kernels, body(): pl.pallas_call(kernel, out_shape=tuple((vm(*shape) for shape in shapes)),...  64.2 us
    pallas_call x1, Pallas kernels, body(): pl.pallas_call(store_kernel, out_shape=tuple((jax.ShapeDtypeStruct(*shape...  3.77 us

profile of v3, /device:TPU:1, one launch (start us, length us, event | category | flops | bytes accessed | tf_op | source)
XLA Modules:
  0.0 68.8 jit_solution(17194357259206104298)
XLA Ops:
  0.6 64.2 %shard_map.84 = (bf16[4,256,1280]{2,1,0:T(8,128)(2,1)S(1)}, f32[8,8,1280]{2,1,0:T(8,128)S(1)}, bf16[640,2560]{1,0:T(8,128)(2,1)S(1)}, bf16[1280,1280]{1,0:T(8,128)(2,1)S(1)}) custom-call(bf16[4,256,1280]{2,1,0:T(8,128)(2,1)} %tok_hbm.1, bf16[64,1280]{1,0:T(8,128)(2,1)} %bitcast.10, bf16[1280,2560]{1,0:T(8,128)(2,1)} %bitcast.8, bf16[2560,1280]{1,0:T(8,128)(2,1)} %bitcast.9, ...), custom_call_target="tpu_custom_call" | custom-call | tf_op jit(solution)/shard_map/pallas_call | solution.py:450
  64.9 3.8 %shard_map.85 = (bf16[4,256,1280]{2,1,0:T(8,128)(2,1)}, f32[8,8,1280]{2,1,0:T(8,128)}, bf16[640,2560]{1,0:T(8,128)(2,1)}, bf16[1280,1280]{1,0:T(8,128)(2,1)}) custom-call(bf16[4,256,1280]{2,1,0:T(8,128)(2,1)S(1)} %get-tuple-element.12.refs_0_, f32[8,8,1280]{2,1,0:T(8,128)S(1)} %get-tuple-element.13.refs_1_, bf16[640,2560]{1,0:T(8,128)(2,1)S(1)} %get-tuple-element.14.refs_2_, ...), custom_call_target="tpu_custom_call" | custom-call | tf_op jit(solution)/shard_map/pallas_call | solution.py:460

commit v4 on v3

--- a/solution.py
+++ b/solution.py
@@ -326,12 +326,6 @@
         dlm[:, b * M : (b + 1) * M] = jnp.where(image == b, d_logits, 0.0).astype(BF)
     per_slot = dot(pick_t, dlm[...]).astype(BF)
 
-    for q in range(4):
-        width = min(PIECE, D - q * PIECE)
-        rhs = tok[:, :, q * PIECE : q * PIECE + width].reshape(B * M, width)
-        gp[:, :, q, :, :width] = dot(per_slot, rhs).reshape(2, 4, 8, width)
-    gp[:, :, 3, :, width:] = jnp.zeros((2, 4, 8, PIECE - width), F32)
-
     zc = zh * 2 + r
     sibling = device(zh, r, x, y, 1 - c)
 
@@ -363,9 +357,14 @@
             right = jnp.concatenate([ys[1, :, cols], wrep[:, cols]], axis=0)
             gt_out[b, :, cols] = dot(left, right).astype(BF)
 
-    to_core = remote(gp.at[1 - c], cbuf, 0, sibling)
-    to_core.start()
-    to_core.wait_recv()
+    for q in range(4):
+        width = min(PIECE, D - q * PIECE)
+        rhs = tok[:, :, q * PIECE : q * PIECE + width].reshape(B * M, width)
+        gp[:, :, q, :, :width] = dot(per_slot, rhs).reshape(2, 4, 8, width)
+        if width < PIECE:
+            gp[:, :, q, :, width:] = jnp.zeros((2, 4, 8, PIECE - width), F32)
+        remote(gp.at[1 - c, :, q], cbuf.at[:, q], 0, sibling).start()
+    wait_parts(cbuf, 4, ar_r.at[0])
     mine[...] = gp[c] + cbuf[...]
     for d in plane_far:
         xx, yy, dev = plane(d)
@@ -405,7 +404,7 @@
     for half in range(2):
         wait_half(half, msg, ssem)
         wait_half(half, msg2, ssem2)
-    to_core.wait_send()
+    wait_parts(cbuf, 4, ar_s.at[0])
     wait_parts(rs, 15, ar_s.at[1])
     wait_parts(zbuf, 3, ar_s.at[2])
     wait_parts(whole, 31, ar_s.at[3])

time: 68.9 us -> 68.9 us (level)
  no operation moved by 1% of the time
where the time goes in v4:
time: 68.9 us; the launch traced here: 68.8 us
  Pallas kernels  68 us (99%)
  between operations  0.82 us (1%)
    pallas_call x1, Pallas kernels, body(): pl.pallas_call(kernel, out_shape=tuple((vm(*shape) for shape in shapes)),...  64.2 us
    pallas_call x1, Pallas kernels, body(): pl.pallas_call(store_kernel, out_shape=tuple((jax.ShapeDtypeStruct(*shape...  3.77 us

profile of v4, /device:TPU:1, one launch (start us, length us, event | category | flops | bytes accessed | tf_op | source)
XLA Modules:
  0.0 68.8 jit_solution(11595510622324241191)
XLA Ops:
  0.6 64.2 %shard_map.84 = (bf16[4,256,1280]{2,1,0:T(8,128)(2,1)S(1)}, f32[8,8,1280]{2,1,0:T(8,128)S(1)}, bf16[640,2560]{1,0:T(8,128)(2,1)S(1)}, bf16[1280,1280]{1,0:T(8,128)(2,1)S(1)}) custom-call(bf16[4,256,1280]{2,1,0:T(8,128)(2,1)} %tok_hbm.1, bf16[64,1280]{1,0:T(8,128)(2,1)} %bitcast.10, bf16[1280,2560]{1,0:T(8,128)(2,1)} %bitcast.8, bf16[2560,1280]{1,0:T(8,128)(2,1)} %bitcast.9, ...), custom_call_target="tpu_custom_call" | custom-call | tf_op jit(solution)/shard_map/pallas_call | solution.py:449
  64.9 3.8 %shard_map.85 = (bf16[4,256,1280]{2,1,0:T(8,128)(2,1)}, f32[8,8,1280]{2,1,0:T(8,128)}, bf16[640,2560]{1,0:T(8,128)(2,1)}, bf16[1280,1280]{1,0:T(8,128)(2,1)}) custom-call(bf16[4,256,1280]{2,1,0:T(8,128)(2,1)S(1)} %get-tuple-element.12.refs_0_, f32[8,8,1280]{2,1,0:T(8,128)S(1)} %get-tuple-element.13.refs_1_, bf16[640,2560]{1,0:T(8,128)(2,1)S(1)} %get-tuple-element.14.refs_2_, ...), custom_call_target="tpu_custom_call" | custom-call | tf_op jit(solution)/shard_map/pallas_call | solution.py:459
